TPU v7x, 32 devices: a whole 2x2x4 slice. The times are simulated.
32 devices in a mesh: band: 16 (over z, x, core), mem: 2 (over y).
Axes of the slice: x: 2, y: 2, z: 4, core: 2. Of those that a mesh axis runs over, the one named last changes fastest.
Arguments:
- spectra: bfloat16 [4, 4, 2, 2, 901120], P('mem', None, None, None, 'band'), may hold values from -6 to 6
- legendre: bfloat16 [10, 901120], P(None, 'band'), may hold values from -0.0034179688 to 0.0034179688
- pair_waves: int32 [640], P('band'), may hold values from 0 to 639, each once
- band_lengths: int32 [16], replicated, may hold values from 1 to 2, 20 in all
- eof_basis: bfloat16 [32, 2560, 256], P('band'), may hold values from -0.0390625 to 0.0390625
Outputs:
- grid_fields: bfloat16 [4, 4, 2, 32, 2560], P('mem', None, None, 'band')
- eof_coeffs: float32 [4, 4, 2, 256], P('mem', None, None, 'band')
Inputs may be any that keep to these rules, and one draw needn't show every extreme that they name: `pair_waves`: every lower wavenumber 0 .. 639 stands in exactly one pair slot. `band_lengths`: the lengths sum to 20; some band has exactly 2 rows.
All inputs are finite; a program needn't handle non-finite values.
Results may differ from a plain program's by a relative error of at most 0.0055.
Values may be sent and summed in bfloat16 or wider, within the bound.
A program may use at most 192 MiB of HBM per device.

v0:
```python
import math

import jax
import jax.numpy as jnp
import ml_dtypes
import numpy as np
from jax import lax
from jax.experimental import pallas as pl
from jax.experimental.pallas import tpu as pltpu
from jax.sharding import PartitionSpec as P

WAVE_COUNT = 1280
BLK = 128
HALF = WAVE_COUNT // 2
F32 = jnp.float32
BF16 = jnp.bfloat16
VMEM_LIMIT = 48 * 1024 * 1024
LEGENDRE_VMEM = 62 * 1024 * 1024


def iota(shape, axis):
    return lax.broadcasted_iota(jnp.int32, shape, axis)


def round_up(number, multiple):
    return -(-number // multiple) * multiple


def group_of(count, most):
    return max(size for size in range(1, most + 1) if count % size == 0)


def row_of(scalars, count, width):
    lane = iota((1, width), 1)
    values = jnp.zeros((1, width), jnp.int32)
    for index in range(count):
        values = jnp.where(lane == index, scalars[index], values)
    return values


def legendre_kernel(
    waves_smem, lengths_smem, spectra_ref, legendre_ref, out_ref, select_ref, total_ref,
    *, group, lat_half, lat_pad, bands, rows, pairs,
):
    step = pl.program_id(0)
    pair_len = legendre_ref.shape[1] // group
    fields = spectra_ref.shape[0]
    columns = 2 * fields
    width = 2 * rows * columns

    @pl.when(step == 0)
    def _():
        shape = (2 * rows * bands, 4 * lat_pad)
        slot = iota((2 * rows * bands, bands), 0)
        band = slot % bands
        lane = iota((2 * rows * bands, bands), 1)
        lengths = row_of(lengths_smem, bands, bands)
        start = jnp.sum(jnp.where(lane < band, lengths, 0).astype(F32), axis=1, keepdims=True)
        own = jnp.sum(jnp.where(lane == band, lengths, 0).astype(F32), axis=1, keepdims=True)
        slot = iota(shape, 0)
        row = slot // bands % rows
        place = iota(shape, 1)
        lat = jnp.broadcast_to(start, shape).astype(jnp.int32) + row
        keep = row < jnp.broadcast_to(own, shape).astype(jnp.int32)
        wanted = jnp.where(lat < lat_half, lat, lat_pad + 2 * lat_half - 1 - lat)
        wanted = wanted + slot // (bands * rows) * (2 * lat_pad)
        select_ref[...] = jnp.where(keep & (place == wanted), 1.0, 0.0).astype(BF16)

    widen = (iota((lat_pad, lat_half), 0) == iota((lat_pad, lat_half), 1)).astype(BF16)
    position = iota((lat_pad, pair_len), 1)
    sign = jnp.where(position % 2 == 0, 1.0, -1.0)
    lane_in = iota((width, width), 0)
    lane_out = iota((width, width), 1)
    block, rest = lane_in // columns, lane_in % columns
    target = ((block // rows * 2 + rest % 2) * rows + block % rows) * fields + rest // 2
    reorder = (lane_out == target).astype(BF16)
    north = jnp.dot(widen, legendre_ref[...], preferred_element_type=F32)
    sums = []
    for index in range(group):
        span = slice(index * pair_len, (index + 1) * pair_len)
        lower = waves_smem[step * group + index]
        high_start = WAVE_COUNT - lower // BLK * BLK
        low = position < WAVE_COUNT - lower
        high = (position >= high_start) & (position < high_start + lower + 1)
        low_part = jnp.where(low, north[:, span], 0.0)
        high_part = jnp.where(high, north[:, span], 0.0)
        weights = jnp.concatenate(
            [low_part, low_part * sign, high_part, high_part * sign], axis=0
        ).astype(BF16)
        coeffs = spectra_ref[:, :, span].reshape(columns, pair_len)
        sums.append(
            lax.dot_general(coeffs, weights, (((1,), (1,)), ((), ())), preferred_element_type=F32)
        )
    fourier = jnp.concatenate(sums, axis=0).astype(BF16)
    picked = lax.dot_general(
        select_ref[...], fourier, (((1,), (1,)), ((), ())), preferred_element_type=F32
    )
    wide = jnp.concatenate(
        [
            jnp.concatenate(
                [
                    picked[i * bands : (i + 1) * bands, index * columns : (index + 1) * columns]
                    for i in range(2 * rows)
                ],
                axis=1,
            )
            for index in range(group)
        ],
        axis=0,
    ).astype(BF16)
    wide = jnp.dot(wide, reorder, preferred_element_type=F32).reshape(group, bands, width)
    total_ref[pl.ds(step * group, group)] = wide

    @pl.when(step == pl.num_programs(0) - 1)
    def _():
        pad = out_ref.shape[1] - pairs
        waves = row_of(waves_smem, pairs, width)
        kind = iota((pad, width), 0)
        extra = jnp.where(
            kind == 0, (waves // BLK).astype(F32), jnp.where(kind == 1, (waves % BLK).astype(F32), 0.0)
        )
        total = jnp.swapaxes(total_ref[...], 0, 1)
        extra = jnp.broadcast_to(extra[None], (bands, pad, width))
        out_ref[...] = jnp.concatenate([total, extra], axis=1).astype(BF16)


def synthesis_kernel(
    payload_ref, table_ref, first_eof_ref, last_eof_ref, grid_ref, anomaly_ref,
    arrived_ref, waves_in_ref, projection_ref, shares_ref, shares_in_ref, members_ref,
    send_sem, recv_sem, share_send_sem, share_recv_sem, mem_send_sem, mem_recv_sem, local_sem,
    *, bands, mems, members, rows, pairs,
):
    step = pl.program_id(0)
    steps = pl.num_programs(0)
    taken = payload_ref.shape[1]
    width = payload_ref.shape[2]
    fields = width // (4 * rows)
    me = lax.axis_index("band")
    my_mem = lax.axis_index("mem")
    share = shares_ref.shape[1]

    def band_copies(source, landing, sends, receives):
        copies = []
        for hop in range(1, bands):
            peer = lax.rem(me + hop, bands)
            copies.append(
                pltpu.make_async_remote_copy(
                    src_ref=source.at[peer],
                    dst_ref=landing.at[me],
                    send_sem=sends.at[hop],
                    recv_sem=receives.at[hop],
                    device_id=(peer, my_mem),
                    device_id_type=pl.DeviceIdType.MESH,
                )
            )
        return copies

    @pl.when(step == 0)
    def _():
        barrier = pltpu.get_barrier_semaphore()
        for hop in range(1, bands):
            pl.semaphore_signal(
                barrier, inc=1, device_id=(lax.rem(me + hop, bands), my_mem),
                device_id_type=pl.DeviceIdType.MESH,
            )
        for hop in range(1, mems):
            pl.semaphore_signal(
                barrier, inc=1, device_id=(me, lax.rem(my_mem + hop, mems)),
                device_id_type=pl.DeviceIdType.MESH,
            )
        local = pltpu.make_async_copy(payload_ref.at[me], arrived_ref.at[me], local_sem)
        local.start()
        pl.semaphore_wait(barrier, bands + mems - 2)
        copies = band_copies(payload_ref, arrived_ref, send_sem, recv_sem)
        for copy in copies:
            copy.start()
        projection_ref[...] = jnp.zeros_like(projection_ref)
        local.wait()
        for copy in copies:
            copy.wait()
        count = bands * taken
        arrived = arrived_ref[...]
        coded = arrived.astype(F32)
        high = jnp.sum(jnp.where(iota(coded.shape, 1) == pairs, coded, 0.0), axis=1)
        low = jnp.sum(jnp.where(iota(coded.shape, 1) == pairs + 1, coded, 0.0), axis=1)
        waves = high * BLK + low
        waves = jnp.broadcast_to(waves[:, None, :], (bands, taken, width))
        slot = iota(waves.shape, 1)
        lane = iota(waves.shape, 2)
        own = jnp.sum(jnp.where(slot == lane, waves, 0.0), axis=2, keepdims=True)
        own = jnp.where(iota(own.shape, 1) < pairs, own, -1.0).reshape(count, 1)
        place = iota((count, HALF), 1)
        order = jnp.where(place < HALF // 2, 2 * place, 2 * place - (HALF - 1)).astype(F32)
        match = jnp.where(own == order, 1.0, 0.0).astype(BF16)
        ordered = lax.dot_general(
            arrived.reshape(count, width), match, (((0,), (0,)), ((), ())), preferred_element_type=F32
        )
        quarter = rows * fields
        first_half = iota((2 * quarter, HALF), 1) < HALF // 2
        low_order, high_order = ordered[: 2 * quarter], ordered[2 * quarter :]
        waves_in_ref[0] = jnp.where(first_half, low_order, high_order).astype(BF16)
        waves_in_ref[1] = jnp.where(first_half, high_order, low_order).astype(BF16)

    quarter = rows * fields
    even, odd = (
        jnp.dot(waves_in_ref[parity, :quarter], table_ref[parity, 0], preferred_element_type=F32)
        + jnp.dot(waves_in_ref[parity, quarter:], table_ref[parity, 1], preferred_element_type=F32)
        for parity in range(2)
    )
    total = projection_ref[...]
    lon_width = even.shape[1]
    for base, eof, value in ((0, first_eof_ref, even + odd), (steps, last_eof_ref, even - odd)):
        parts = [value[row * fields : (row + 1) * fields] for row in range(rows)]
        span = pl.ds(pl.multiple_of((base + step) * lon_width, lon_width), lon_width)
        grid_ref[:, :, span] = jnp.stack(parts, axis=1).astype(BF16)
        for row in range(rows):
            total += lax.dot_general(
                eof[row], parts[row].astype(BF16), (((0,), (1,)), ((), ())), preferred_element_type=F32
            )
    projection_ref[...] = total

    @pl.when(step == steps - 1)
    def _():
        shares_ref[...] = projection_ref[...].reshape(bands, share, fields)
        copies = band_copies(shares_ref, shares_in_ref, share_send_sem, share_recv_sem)
        for copy in copies:
            copy.start()
        shares_in_ref[me] = shares_ref[me]
        for copy in copies:
            copy.wait()
        own = jnp.sum(shares_in_ref[...], axis=0)
        members_ref[my_mem] = own
        copies = []
        for hop in range(1, mems):
            peer = lax.rem(my_mem + hop, mems)
            copies.append(
                pltpu.make_async_remote_copy(
                    src_ref=members_ref.at[my_mem],
                    dst_ref=members_ref.at[my_mem],
                    send_sem=mem_send_sem.at[hop],
                    recv_sem=mem_recv_sem.at[hop],
                    device_id=(me, peer),
                    device_id_type=pl.DeviceIdType.MESH,
                )
            )
        for copy in copies:
            copy.start()
        for copy in copies:
            copy.wait()
        total = jnp.sum(members_ref[...], axis=0)
        stack = fields // members
        mean = sum(total[:, i * stack : (i + 1) * stack] for i in range(members)) / (members * mems)
        anomaly_ref[...] = own - jnp.concatenate([mean] * members, axis=1)


def wave_tables(longitudes):
    place = np.arange(HALF)
    lower = np.where(place < HALF // 2, 2 * place, 2 * place - (HALF - 1))
    upper = WAVE_COUNT - 1 - lower
    even = np.where(lower % 2 == 0, lower, upper)
    orders = np.stack([even, WAVE_COUNT - 1 - even])
    phase = orders[..., None] * np.arange(longitudes // 2) % longitudes
    angle = phase * (2.0 * math.pi / longitudes)
    weight = np.where(orders == 0, 1.0, 2.0)[..., None]
    table = np.stack([weight * np.cos(angle), -weight * np.sin(angle)], axis=1)
    return table.astype(np.float32).astype(ml_dtypes.bfloat16)


def shards(spectra, legendre, pair_waves, band_lengths, eof_basis):
    members, fields, levels, re_im, slot_count = spectra.shape
    lat_half = legendre.shape[0]
    pairs = pair_waves.shape[0]
    pair_len = slot_count // pairs
    stack = members * fields * levels
    bands = lax.axis_size("band")
    rows, longitudes, modes = eof_basis.shape
    width = 2 * rows * stack * re_im
    group = group_of(pairs, 8)
    lat_pad = round_up(lat_half, 16)
    taken = round_up(pairs + 2, 16)
    mems = lax.axis_size("mem")

    def fixed(*shape):
        return pl.BlockSpec(shape, lambda *_: (0,) * len(shape))

    payload = pl.pallas_call(
        lambda *refs: legendre_kernel(
            *refs, group=group, lat_half=lat_half, lat_pad=lat_pad, bands=bands, rows=rows, pairs=pairs
        ),
        out_shape=jax.ShapeDtypeStruct((bands, taken, width), BF16),
        grid_spec=pltpu.PrefetchScalarGridSpec(
            num_scalar_prefetch=2,
            grid=(pairs // group,),
            in_specs=[
                pl.BlockSpec((stack, re_im, group * pair_len), lambda i, *_: (0, 0, i)),
                pl.BlockSpec((lat_half, group * pair_len), lambda i, *_: (0, i)),
            ],
            out_specs=fixed(bands, taken, width),
            scratch_shapes=[
                pltpu.VMEM((2 * rows * bands, 4 * lat_pad), BF16),
                pltpu.VMEM((pairs, bands, width), F32),
            ],
        ),
        compiler_params=pltpu.CompilerParams(vmem_limit_bytes=LEGENDRE_VMEM),
        name="legendre",
    )(pair_waves, band_lengths, spectra.reshape(stack, re_im, slot_count), legendre)
    lon_width = math.gcd(longitudes // 2, 256)
    steps = longitudes // 2 // lon_width
    table = jnp.asarray(wave_tables(longitudes))
    share = modes // bands
    dma = pltpu.SemaphoreType.DMA
    grid, anomaly = pl.pallas_call(
        lambda *refs: synthesis_kernel(
            *refs, bands=bands, mems=mems, members=members, rows=rows, pairs=pairs
        ),
        out_shape=(
            jax.ShapeDtypeStruct((stack, rows, longitudes), BF16),
            jax.ShapeDtypeStruct((share, stack), F32),
        ),
        grid=(steps,),
        in_specs=[
            fixed(bands, taken, width),
            pl.BlockSpec((2, 2, HALF, lon_width), lambda i: (0, 0, 0, i)),
            pl.BlockSpec((rows, lon_width, modes), lambda i: (0, i, 0)),
            pl.BlockSpec((rows, lon_width, modes), lambda i: (0, i + steps, 0)),
        ],
        out_specs=(fixed(stack, rows, longitudes), fixed(share, stack)),
        scratch_shapes=[
            pltpu.VMEM((bands, taken, width), BF16),
            pltpu.VMEM((2, 2 * rows * stack, HALF), BF16),
            pltpu.VMEM((modes, stack), F32),
            pltpu.VMEM((bands, share, stack), F32),
            pltpu.VMEM((bands, share, stack), F32),
            pltpu.VMEM((mems, share, stack), F32),
            dma((bands,)),
            dma((bands,)),
            dma((bands,)),
            dma((bands,)),
            dma((mems,)),
            dma((mems,)),
            dma,
        ],
        compiler_params=pltpu.CompilerParams(
            vmem_limit_bytes=VMEM_LIMIT, collective_id=0, has_side_effects=True
        ),
        name="synthesis",
    )(payload, table, eof_basis, eof_basis)
    grid_fields = grid.reshape(members, fields, levels, rows, longitudes)
    return (grid_fields, anomaly.T.reshape(members, fields, levels, share))


def solution(mesh):
    return jax.shard_map(
        shards,
        mesh=mesh,
        in_specs=(
            P("mem", None, None, None, "band"),
            P(None, "band"),
            P("band"),
            P(),
            P("band", None, None),
        ),
        out_specs=(P("mem", None, None, "band", None), P("mem", None, None, "band")),
        check_vma=False,
    )
```

profile of v0, /device:TPU:0, one launch (start us, length us, event | category | flops | bytes accessed | tf_op | source)
XLA Modules:
  0.0 40.2 jit_solution(10097829882990349150)
XLA Ops:
  0.6 8.6 %legendre.1.refs_0_ = bf16[16,48,128]{2,1,0:T(8,128)(2,1)} custom-call(s32[40]{0:T(128)} %refs_0_.1, s32[16]{0:T(128)} %refs_1_.2, bf16[16,2,56320]{2,1,0:T(2,128)(2,1)} %bitcast.6, bf16[10,56320]{1,0:T(8,128)(2,1)} %refs_3_.2), custom_call_target="tpu_custom_call" | custom-call | tf_op jit(solution)/shard_map/legendre/pallas_call | solution.py:286
  9.3 0.0 copy-start
  9.3 1.7 %copy-done = bf16[2,2560,256]{2,1,0:T(8,128)(2,1)S(1)} copy-done((bf16[2,2560,256]{2,1,0:T(8,128)(2,1)S(1)}, bf16[2,2560,256]{2,1,0:T(8,128)(2,1)}, u32[]{:S(2)}) %copy-start) | copy-done | bytes 2621464
  11.0 0.0 copy-start.1
  11.0 0.9 %copy-done.1 = bf16[16,48,128]{2,1,0:T(8,128)(2,1)S(1)} copy-done((bf16[16,48,128]{2,1,0:T(8,128)(2,1)S(1)}, bf16[16,48,128]{2,1,0:T(8,128)(2,1)}, u32[]{:S(2)}) %copy-start.1) | copy-done | bytes 196632
  11.9 27.0 %synthesis.1 = (bf16[16,2,2560]{2,1,0:T(2,128)(2,1)S(1)}, f32[16,16]{1,0:T(8,128)S(1)}) custom-call(bf16[16,48,128]{2,1,0:T(8,128)(2,1)S(1)} %copy-done.1, bf16[2,2,640,1280]{3,2,1,0:T(8,128)(2,1)} %constant.2.clone.refs_1_, bf16[2,2560,256]{2,1,0:T(8,128)(2,1)S(1)} %copy-done, bf16[2,2560,256]{2,1,0:T(8,128)(2,1)S(1)} %copy-done), custom_call_target="tpu_custom_call" | custom-call | tf_op jit(solution)/shard_map/synthesis/pallas_call | solution.py:312
  38.9 0.7 %copy.9 = f32[16,16]{1,0:T(8,128)} copy(f32[16,16]{0,1:T(8,128)S(1)} %bitcast.5) | data formatting | bytes 2048 | tf_op jit(solution)/shard_map/transpose | solution.py:349
  39.6 0.7 %copy.11 = bf16[2,4,2,2,2560]{4,3,2,1,0:T(2,128)(2,1)} copy(bf16[2,4,2,2,2560]{4,3,2,1,0:T(2,128)(2,1)S(1)} %bitcast.4) | data formatting | bytes 327680
Async XLA Ops:
  9.3 1.7 %copy-start = (bf16[2,2560,256]{2,1,0:T(8,128)(2,1)S(1)}, bf16[2,2560,256]{2,1,0:T(8,128)(2,1)}, u32[]{:S(2)}) copy-start(bf16[2,2560,256]{2,1,0:T(8,128)(2,1)} %refs_3_.3) | copy-start | bytes 7864324
  11.0 0.9 %copy-start.1 = (bf16[16,48,128]{2,1,0:T(8,128)(2,1)S(1)}, bf16[16,48,128]{2,1,0:T(8,128)(2,1)}, u32[]{:S(2)}) copy-start(bf16[16,48,128]{2,1,0:T(8,128)(2,1)} %legendre.1.refs_0_) | copy-start | bytes 589828
where the time goes:
time: 40.6 us; the launch traced here: 40.2 us
  Pallas kernels  35.6 us (88%)
  local copies, waits for them, and re-layouts  4 us (10%)
  between operations  0.64 us (2%)
    pallas_call x1, Pallas kernels, shards(): pl.pallas_call(lambda *refs: synthesis_kernel(*refs, bands=bands, mems=me...  27 us
    pallas_call x1, Pallas kernels, shards(): pl.pallas_call(lambda *refs: legendre_kernel(*refs, group=group, lat_half...  8.63 us
    unnamed x5, local copies, waits for them, and re-layouts  3.33 us

commit v1 on v0

v1 whole, which is shorter than its diff:
```python
import math

import jax
import jax.numpy as jnp
import ml_dtypes
import numpy as np
from jax import lax
from jax.experimental import pallas as pl
from jax.experimental.pallas import tpu as pltpu
from jax.sharding import PartitionSpec as P

WAVE_COUNT = 1280
BLK = 128
HALF = WAVE_COUNT // 2
F32 = jnp.float32
BF16 = jnp.bfloat16
VMEM_LIMIT = 62 * 1024 * 1024


def iota(shape, axis):
    return lax.broadcasted_iota(jnp.int32, shape, axis)


def round_up(number, multiple):
    return -(-number // multiple) * multiple


def group_of(count, most):
    return max(size for size in range(1, most + 1) if count % size == 0)


def row_of(scalars, count, width):
    lane = iota((1, width), 1)
    values = jnp.zeros((1, width), jnp.int32)
    for index in range(count):
        values = jnp.where(lane == index, scalars[index], values)
    return values


def transform_kernel(
    waves_smem, lengths_smem, spectra_ref, legendre_ref, table_hbm, eof_hbm, grid_ref, anomaly_ref,
    select_ref, total_ref, payload_ref, arrived_ref, waves_in_ref, projection_ref,
    shares_ref, shares_in_ref, members_ref, table_ref, eof_ref,
    send_sem, recv_sem, share_send_sem, share_recv_sem, mem_send_sem, mem_recv_sem, local_sem,
    *, group, lat_half, lat_pad, bands, mems, members, rows, pairs, lon_width,
):
    step = pl.program_id(0)
    steps = pl.num_programs(0)
    pair_steps = pairs // group
    pair_len = legendre_ref.shape[1] // group
    fields = spectra_ref.shape[0]
    columns = 2 * fields
    width = 2 * rows * columns
    quarter = rows * fields
    taken = payload_ref.shape[1]
    me = lax.axis_index("band")
    my_mem = lax.axis_index("mem")
    table_copy = pltpu.make_async_copy(table_hbm, table_ref, local_sem.at[0])
    eof_copy = pltpu.make_async_copy(eof_hbm, eof_ref, local_sem.at[1])

    def band_copies(source, landing, sends, receives):
        copies = []
        for hop in range(1, bands):
            peer = lax.rem(me + hop, bands)
            copies.append(
                pltpu.make_async_remote_copy(
                    src_ref=source.at[peer],
                    dst_ref=landing.at[me],
                    send_sem=sends.at[hop],
                    recv_sem=receives.at[hop],
                    device_id=(peer, my_mem),
                    device_id_type=pl.DeviceIdType.MESH,
                )
            )
        return copies

    @pl.when(step == 0)
    def _():
        barrier = pltpu.get_barrier_semaphore()
        for hop in range(1, bands):
            pl.semaphore_signal(
                barrier, inc=1, device_id=(lax.rem(me + hop, bands), my_mem),
                device_id_type=pl.DeviceIdType.MESH,
            )
        for hop in range(1, mems):
            pl.semaphore_signal(
                barrier, inc=1, device_id=(me, lax.rem(my_mem + hop, mems)),
                device_id_type=pl.DeviceIdType.MESH,
            )
        table_copy.start()
        eof_copy.start()
        shape = (2 * rows * bands, 4 * lat_pad)
        slot = iota((2 * rows * bands, bands), 0)
        band = slot % bands
        lane = iota((2 * rows * bands, bands), 1)
        lengths = row_of(lengths_smem, bands, bands)
        start = jnp.sum(jnp.where(lane < band, lengths, 0).astype(F32), axis=1, keepdims=True)
        own = jnp.sum(jnp.where(lane == band, lengths, 0).astype(F32), axis=1, keepdims=True)
        slot = iota(shape, 0)
        row = slot // bands % rows
        place = iota(shape, 1)
        lat = jnp.broadcast_to(start, shape).astype(jnp.int32) + row
        keep = row < jnp.broadcast_to(own, shape).astype(jnp.int32)
        wanted = jnp.where(lat < lat_half, lat, lat_pad + 2 * lat_half - 1 - lat)
        wanted = wanted + slot // (bands * rows) * (2 * lat_pad)
        select_ref[...] = jnp.where(keep & (place == wanted), 1.0, 0.0).astype(BF16)

    @pl.when(step < pair_steps)
    def _():
        widen = (iota((lat_pad, lat_half), 0) == iota((lat_pad, lat_half), 1)).astype(BF16)
        position = iota((lat_pad, pair_len), 1)
        sign = jnp.where(position % 2 == 0, 1.0, -1.0)
        lane_in = iota((width, width), 0)
        lane_out = iota((width, width), 1)
        block, rest = lane_in // columns, lane_in % columns
        target = ((block // rows * 2 + rest % 2) * rows + block % rows) * fields + rest // 2
        reorder = (lane_out == target).astype(BF16)
        north = jnp.dot(widen, legendre_ref[...], preferred_element_type=F32)
        sums = []
        for index in range(group):
            span = slice(index * pair_len, (index + 1) * pair_len)
            lower = waves_smem[step * group + index]
            high_start = WAVE_COUNT - lower // BLK * BLK
            low = position < WAVE_COUNT - lower
            high = (position >= high_start) & (position < high_start + lower + 1)
            low_part = jnp.where(low, north[:, span], 0.0)
            high_part = jnp.where(high, north[:, span], 0.0)
            weights = jnp.concatenate(
                [low_part, low_part * sign, high_part, high_part * sign], axis=0
            ).astype(BF16)
            coeffs = spectra_ref[:, :, span].reshape(columns, pair_len)
            sums.append(
                lax.dot_general(coeffs, weights, (((1,), (1,)), ((), ())), preferred_element_type=F32)
            )
        fourier = jnp.concatenate(sums, axis=0).astype(BF16)
        picked = lax.dot_general(
            select_ref[...], fourier, (((1,), (1,)), ((), ())), preferred_element_type=F32
        )
        wide = jnp.concatenate(
            [
                jnp.concatenate(
                    [
                        picked[i * bands : (i + 1) * bands, index * columns : (index + 1) * columns]
                        for i in range(2 * rows)
                    ],
                    axis=1,
                )
                for index in range(group)
            ],
            axis=0,
        ).astype(BF16)
        wide = jnp.dot(wide, reorder, preferred_element_type=F32).reshape(group, bands, width)
        total_ref[pl.ds(step * group, group)] = wide

    @pl.when(step == pair_steps - 1)
    def _():
        pad = payload_ref.shape[1] - pairs
        waves = row_of(waves_smem, pairs, width)
        kind = iota((pad, width), 0)
        extra = jnp.where(
            kind == 0, (waves // BLK).astype(F32), jnp.where(kind == 1, (waves % BLK).astype(F32), 0.0)
        )
        total = jnp.swapaxes(total_ref[...], 0, 1)
        extra = jnp.broadcast_to(extra[None], (bands, pad, width))
        payload_ref[...] = jnp.concatenate([total, extra], axis=1).astype(BF16)
        pl.semaphore_wait(pltpu.get_barrier_semaphore(), bands + mems - 2)
        copies = band_copies(payload_ref, arrived_ref, send_sem, recv_sem)
        for copy in copies:
            copy.start()
        arrived_ref[me] = payload_ref[me]
        projection_ref[...] = jnp.zeros_like(projection_ref)
        for copy in copies:
            copy.wait()
        count = bands * taken
        arrived = arrived_ref[...]
        coded = arrived.astype(F32)
        high = jnp.sum(jnp.where(iota(coded.shape, 1) == pairs, coded, 0.0), axis=1)
        low = jnp.sum(jnp.where(iota(coded.shape, 1) == pairs + 1, coded, 0.0), axis=1)
        waves = high * BLK + low
        waves = jnp.broadcast_to(waves[:, None, :], (bands, taken, width))
        slot = iota(waves.shape, 1)
        lane = iota(waves.shape, 2)
        own = jnp.sum(jnp.where(slot == lane, waves, 0.0), axis=2, keepdims=True)
        own = jnp.where(iota(own.shape, 1) < pairs, own, -1.0).reshape(count, 1)
        place = iota((count, HALF), 1)
        order = jnp.where(place < HALF // 2, 2 * place, 2 * place - (HALF - 1)).astype(F32)
        match = jnp.where(own == order, 1.0, 0.0).astype(BF16)
        ordered = lax.dot_general(
            arrived.reshape(count, width), match, (((0,), (0,)), ((), ())), preferred_element_type=F32
        )
        first_half = iota((2 * quarter, HALF), 1) < HALF // 2
        low_order, high_order = ordered[: 2 * quarter], ordered[2 * quarter :]
        waves_in_ref[0] = jnp.where(first_half, low_order, high_order).astype(BF16)
        waves_in_ref[1] = jnp.where(first_half, high_order, low_order).astype(BF16)
        table_copy.wait()
        eof_copy.wait()

    @pl.when(step >= pair_steps)
    def _():
        place = step - pair_steps
        span = pl.ds(pl.multiple_of(place * lon_width, lon_width), lon_width)
        even, odd = (
            jnp.dot(
                waves_in_ref[parity, :quarter], table_ref[parity, 0, :, span],
                preferred_element_type=F32,
            )
            + jnp.dot(
                waves_in_ref[parity, quarter:], table_ref[parity, 1, :, span],
                preferred_element_type=F32,
            )
            for parity in range(2)
        )
        total = projection_ref[...]
        for base, value in ((0, even + odd), (steps - pair_steps, even - odd)):
            parts = [value[row * fields : (row + 1) * fields] for row in range(rows)]
            span = pl.ds(pl.multiple_of((base + place) * lon_width, lon_width), lon_width)
            grid_ref[:, :, span] = jnp.stack(parts, axis=1).astype(BF16)
            for row in range(rows):
                total += lax.dot_general(
                    eof_ref[row, span, :], parts[row].astype(BF16), (((0,), (1,)), ((), ())),
                    preferred_element_type=F32,
                )
        projection_ref[...] = total

    @pl.when(step == steps - 1)
    def _():
        fold = shares_ref.shape[2] // fields
        high = shares_ref.shape[1]
        shares = projection_ref[...].reshape(bands, fold * high, fields)
        shares_ref[...] = jnp.concatenate(
            [shares[:, i * high : (i + 1) * high] for i in range(fold)], axis=2
        )
        copies = band_copies(shares_ref, shares_in_ref, share_send_sem, share_recv_sem)
        for copy in copies:
            copy.start()
        shares_in_ref[me] = shares_ref[me]
        for copy in copies:
            copy.wait()
        own = jnp.sum(shares_in_ref[...], axis=0)
        members_ref[my_mem] = own
        copies = []
        for hop in range(1, mems):
            peer = lax.rem(my_mem + hop, mems)
            copies.append(
                pltpu.make_async_remote_copy(
                    src_ref=members_ref.at[my_mem],
                    dst_ref=members_ref.at[my_mem],
                    send_sem=mem_send_sem.at[hop],
                    recv_sem=mem_recv_sem.at[hop],
                    device_id=(me, peer),
                    device_id_type=pl.DeviceIdType.MESH,
                )
            )
        for copy in copies:
            copy.start()
        for copy in copies:
            copy.wait()

        def unfolded(value):
            return jnp.concatenate(
                [value[:, i * fields : (i + 1) * fields] for i in range(fold)], axis=0
            )

        total = unfolded(jnp.sum(members_ref[...], axis=0))
        stack = fields // members
        mean = sum(total[:, i * stack : (i + 1) * stack] for i in range(members)) / (members * mems)
        anomaly_ref[...] = unfolded(own) - jnp.concatenate([mean] * members, axis=1)


def wave_tables(longitudes):
    place = np.arange(HALF)
    lower = np.where(place < HALF // 2, 2 * place, 2 * place - (HALF - 1))
    upper = WAVE_COUNT - 1 - lower
    even = np.where(lower % 2 == 0, lower, upper)
    orders = np.stack([even, WAVE_COUNT - 1 - even])
    phase = orders[..., None] * np.arange(longitudes // 2) % longitudes
    angle = phase * (2.0 * math.pi / longitudes)
    weight = np.where(orders == 0, 1.0, 2.0)[..., None]
    table = np.stack([weight * np.cos(angle), -weight * np.sin(angle)], axis=1)
    return table.astype(np.float32).astype(ml_dtypes.bfloat16)


def shards(spectra, legendre, pair_waves, band_lengths, eof_basis):
    members, fields, levels, re_im, slot_count = spectra.shape
    lat_half = legendre.shape[0]
    pairs = pair_waves.shape[0]
    pair_len = slot_count // pairs
    stack = members * fields * levels
    bands = lax.axis_size("band")
    rows, longitudes, modes = eof_basis.shape
    width = 2 * rows * stack * re_im
    group = group_of(pairs, 8)
    lat_pad = round_up(lat_half, 16)
    taken = round_up(pairs + 2, 16)
    mems = lax.axis_size("mem")

    def fixed(*shape):
        return pl.BlockSpec(shape, lambda *_: (0,) * len(shape))

    lon_width = math.gcd(longitudes // 2, 256)
    pair_steps = pairs // group
    table = wave_tables(longitudes)
    share = modes // bands
    fold = max(1, share // 8)
    folded = (share // fold, fold * stack)
    dma = pltpu.SemaphoreType.DMA
    grid, anomaly = pl.pallas_call(
        lambda *refs: transform_kernel(
            *refs, group=group, lat_half=lat_half, lat_pad=lat_pad, bands=bands, mems=mems,
            members=members, rows=rows, pairs=pairs, lon_width=lon_width,
        ),
        out_shape=(
            jax.ShapeDtypeStruct((stack, rows, longitudes), BF16),
            jax.ShapeDtypeStruct((share, stack), F32),
        ),
        grid=(pair_steps + longitudes // 2 // lon_width,),
        in_specs=[
            pl.BlockSpec(memory_space=pltpu.SMEM),
            pl.BlockSpec(memory_space=pltpu.SMEM),
            pl.BlockSpec(
                (stack, re_im, group * pair_len), lambda i: (0, 0, jnp.minimum(i, pair_steps - 1))
            ),
            pl.BlockSpec((lat_half, group * pair_len), lambda i: (0, jnp.minimum(i, pair_steps - 1))),
            pl.BlockSpec(memory_space=pl.ANY),
            pl.BlockSpec(memory_space=pl.ANY),
        ],
        out_specs=(fixed(stack, rows, longitudes), fixed(share, stack)),
        scratch_shapes=[
            pltpu.VMEM((2 * rows * bands, 4 * lat_pad), BF16),
            pltpu.VMEM((pairs, bands, width), F32),
            pltpu.VMEM((bands, taken, width), BF16),
            pltpu.VMEM((bands, taken, width), BF16),
            pltpu.VMEM((2, 2 * rows * stack, HALF), BF16),
            pltpu.VMEM((modes, stack), F32),
            pltpu.VMEM((bands, *folded), F32),
            pltpu.VMEM((bands, *folded), F32),
            pltpu.VMEM((mems, *folded), F32),
            pltpu.VMEM(table.shape, BF16),
            pltpu.VMEM(eof_basis.shape, BF16),
            dma((bands,)),
            dma((bands,)),
            dma((bands,)),
            dma((bands,)),
            dma((mems,)),
            dma((mems,)),
            dma((2,)),
        ],
        compiler_params=pltpu.CompilerParams(
            vmem_limit_bytes=VMEM_LIMIT, collective_id=0, has_side_effects=True
        ),
        name="transform",
    )(
        pair_waves,
        band_lengths,
        spectra.reshape(stack, re_im, slot_count),
        legendre,
        jnp.asarray(table),
        eof_basis,
    )
    grid_fields = grid.reshape(members, fields, levels, rows, longitudes)
    return (grid_fields, anomaly.T.reshape(members, fields, levels, share))


def solution(mesh):
    return jax.shard_map(
        shards,
        mesh=mesh,
        in_specs=(
            P("mem", None, None, None, "band"),
            P(None, "band"),
            P("band"),
            P(),
            P("band", None, None),
        ),
        out_specs=(P("mem", None, None, "band", None), P("mem", None, None, "band")),
        check_vma=False,
    )
```

time: 40.6 us -> 34.6 us (0.85)
  Pallas kernels: 35.6 us -> 30.7 us
  local copies, waits for them, and re-layouts: 4 us -> 3.06 us
    pallas_call x2 -> x1, Pallas kernels: 35.6 us -> 30.7 us  [shards(): pl.pallas_call(lambda *refs: transform_kernel(*refs, group=group, lat_hal...]
    unnamed x5 -> x1, local copies, waits for them, and re-layouts: 3.33 us -> 1.69 us
    transpose x1, local copies, waits for them, and re-layouts: 0.67 us -> 1.37 us  [shards(): return (grid_fields, anomaly.T.reshape(members, fields, levels, share))]
where the time goes in v1:
time: 34.6 us; the launch traced here: 34.4 us
  Pallas kernels  30.7 us (89%)
  local copies, waits for them, and re-layouts  3.06 us (9%)
  between operations  0.64 us (2%)
    pallas_call x1, Pallas kernels, shards(): pl.pallas_call(lambda *refs: transform_kernel(*refs, group=group, lat_hal...  30.7 us
    unnamed x1, local copies, waits for them, and re-layouts  1.69 us
    transpose x1, local copies, waits for them, and re-layouts, shards(): return (grid_fields, anomaly.T.reshape(members, fields, levels, share))  1.37 us

profile of v1, /device:TPU:0, one launch (start us, length us, event | category | flops | bytes accessed | tf_op | source)
XLA Modules:
  0.0 34.4 jit_solution(7725762372739812937)
XLA Ops:
  0.6 30.7 %transform.1 = (bf16[16,2,2560]{2,1,0:T(2,128)(2,1)}, f32[16,16]{1,0:T(8,128)}) custom-call(s32[40]{0:T(128)} %refs_0_.1, s32[16]{0:T(128)} %refs_1_.1, bf16[16,2,56320]{2,1,0:T(2,128)(2,1)} %bitcast.4, bf16[10,56320]{1,0:T(8,128)(2,1)} %refs_3_.1, bf16[2,2,640,1280]{3,2,1,0:T(8,128)(2,1)} %constant.2.clone.refs_4_, bf16[2,2560,256]{2,1,0:T(8,128)(2,1)} %refs_5_.1), custom_call_target="tpu_custom_call" | custom-call | tf_op jit(solution)/shard_map/transform/pallas_call | solution.py:307
  31.4 1.4 %copy.9 = f32[16,16]{1,0:T(8,128)} copy(f32[16,16]{0,1:T(8,128)} %bitcast.7) | data formatting | bytes 2048 | tf_op jit(solution)/shard_map/transpose | solution.py:361
  32.7 1.7 %copy.11 = bf16[2,4,2,2,2560]{4,3,2,1,0:T(2,128)(2,1)} copy(bf16[2,4,2,2,2560]{4,3,2,1,0:T(2,128)(2,1)} %bitcast.5) | data formatting | bytes 327680
